TPU v7x, 256 devices: a whole 4x4x8 slice. The times are simulated.
256 devices in a mesh: tm: 4 (over y), height: 4 (over x), width: 16 (over z, core).
Axes of the slice: x: 4, y: 4, z: 8, core: 2. Of those that a mesh axis runs over, the one named last changes fastest.
Arguments:
- features: bfloat16 [16, 32, 160, 384], P('tm', 'height', 'width'), may hold values from -6 to 6
- first_gain: float32 [384], replicated, may hold values from 0.5 to 2
- first_kernel: bfloat16 [27, 384, 384], P(None, ('height', 'width')), may hold values from -0.0625 to 0.0625
- first_bias: float32 [384], replicated, may hold values from -3 to 3
- second_gain: float32 [384], replicated, may hold values from 0.5 to 2
- second_kernel: bfloat16 [27, 384, 384], P(None, ('height', 'width')), may hold values from -0.0625 to 0.0625
- second_bias: float32 [384], replicated, may hold values from -3 to 3
Outputs:
- block_out: bfloat16 [16, 32, 160, 384], P('tm', 'height', 'width')
All inputs are finite; a program needn't handle non-finite values.
Results may differ from a plain program's by a relative error of at most 0.012.
Values may be sent and summed in bfloat16 or wider, within the bound.
No kernel may reach another device: no remote copies, remote signals or barrier semaphores. Data moves between devices by JAX's collectives and lax.ppermute only.
A program may use at most 128 MiB of HBM per device.

v0:
```python
import jax
import jax.numpy as jnp
from jax import lax
from jax.sharding import PartitionSpec as P


def passed_along(x, axis, by):
    devices = lax.axis_size(axis)
    pairs = [(i, i + by) for i in range(devices) if 0 <= i + by < devices]
    return lax.ppermute(x, axis, pairs)


def extended(x, sides, width):
    for axis, dim in sides:
        devices, length = (lax.axis_size(axis), x.shape[dim])
        up = [(i, (i + 1) % devices) for i in range(devices - 1)]
        down = [(j, i) for i, j in up]
        last = lax.slice_in_dim(x, length - width, length, axis=dim)
        first = lax.slice_in_dim(x, 0, width, axis=dim)
        before = lax.ppermute(last, axis, up)
        after = lax.ppermute(first, axis, down)
        x = jnp.concatenate([before, x, after], axis=dim)
    return x


def activate(volume, gain):
    values = volume.astype(jnp.float32)
    square_mean = jnp.mean(values * values, axis=-1, keepdims=True)
    normed = values * lax.rsqrt(square_mean + 1e-06) * gain
    return jax.nn.silu(normed).astype(jnp.bfloat16)


def make_folder(widened, frames, rows, cols):

    def fold_piece(total, piece, start):
        count_in = piece.shape[1]
        for step_t in range(3):
            for step_h in range(3):
                for step_w in range(3):
                    window = widened[
                        step_t : step_t + frames, step_h : step_h + rows, step_w : step_w + cols
                    ]
                    total = total + jnp.dot(
                        window.reshape(-1, count_in),
                        piece[9 * step_t + 3 * step_h + step_w],
                        preferred_element_type=jnp.float32,
                    )
        return total

    return fold_piece


def convolve(widened, kernel, bias, frames, rows, cols):
    out_chans = kernel.shape[2]
    empty = jnp.zeros((frames * rows * cols, out_chans), jnp.float32)
    fold_piece = make_folder(widened, frames, rows, cols)
    row_kernel = lax.all_gather(kernel, "width", axis=1, tiled=True)
    total = fold_piece(
        empty, lax.all_gather(row_kernel, "height", axis=1, tiled=True), jnp.int32(0)
    )
    return total.reshape(frames, rows, cols, out_chans) + bias


def widen(active):
    earlier = passed_along(active[-2:], "tm", 1)
    tall = jnp.concatenate([earlier, active], axis=0)
    return extended(tall, (("height", 1), ("width", 2)), 1)


def on_device(
    features, first_gain, first_kernel, first_bias, second_gain, second_kernel, second_bias
):
    frames, rows, cols, chans = features.shape
    first_active = activate(features, first_gain)
    middle = convolve(widen(first_active), first_kernel, first_bias, frames, rows, cols).astype(
        jnp.bfloat16
    )
    second_active = activate(middle, second_gain)
    second_wide = widen(second_active)
    summed = convolve(
        second_wide, second_kernel, second_bias, frames, rows, cols
    ) + features.astype(jnp.float32)
    return summed.astype(jnp.bfloat16)


def solution(mesh):
    placed = (
        P("tm", "height", "width", None),
        P(),
        P(None, ("height", "width"), None),
        P(),
        P(),
        P(None, ("height", "width"), None),
        P(),
    )
    return jax.shard_map(
        on_device,
        mesh=mesh,
        in_specs=placed,
        out_specs=P("tm", "height", "width", None),
        check_vma=False,
    )
```

profile of v0, /device:TPU:1, one launch (start us, length us, event | category | flops | bytes accessed | tf_op | source)
XLA Modules:
  0.0 329.2 jit_solution(13650596367216335500)
XLA Ops:
  8.1 45.3 %all-gather.5.cloned.1.call-done = bf16[27,96,384]{2,0,1:T(8,128)(2,1)} async-done(((bf16[27,6,384]{2,0,1:T(8,128)(2,1)}), bf16[27,96,384]{2,0,1:T(8,128)(2,1)}) %all-gather.5.cloned.1.call-update) | async-done | bytes 1990672 | tf_op jit(solution)/shard_map/all_gather | solution.py:57
  53.4 3.7 %copy.15 = bf16[27,96,384]{2,1,0:T(8,128)(2,1)} copy(bf16[27,96,384]{2,0,1:T(8,128)(2,1)} %all-gather.5.cloned.1.call-done) | data formatting | bytes 3981312 | tf_op jit(solution)/shard_map/all_gather | solution.py:57
  57.1 36.5 %all-gather.9.cloned.1.call-done = bf16[27,96,384]{2,0,1:T(8,128)(2,1)} async-done(((bf16[27,6,384]{2,0,1:T(8,128)(2,1)}), bf16[27,96,384]{2,0,1:T(8,128)(2,1)}) %all-gather.9.cloned.1.call-update) | async-done | bytes 1990672 | tf_op jit(solution)/shard_map/all_gather | solution.py:57
  93.6 3.7 %copy.16 = bf16[27,96,384]{2,1,0:T(8,128)(2,1)} copy(bf16[27,96,384]{2,0,1:T(8,128)(2,1)} %all-gather.9.cloned.1.call-done) | data formatting | bytes 3981312 | tf_op jit(solution)/shard_map/all_gather | solution.py:57
  97.9 3.1 collective-permute-start
  101.8 3.2 collective-permute-done
  106.3 4.0 %collective-permute-start.1 = (bf16[6,1,10,384]{3,2,1,0:T(8,128)(2,1)S(1)}, bf16[6,1,10,384]{3,2,1,0:T(8,128)(2,1)S(1)}, u32[]{:S(2)}, u32[]{:S(2)}) collective-permute-start(bf16[6,1,10,384]{3,2,1,0:T(8,128)(2,1)S(1)} %get-tuple-element.71), channel_id=1, source_target_pairs={{0,16},{16,32},{32,48},{1,17},{17,33},{33,49},{2,18},{18,34},{34,5... | collective-permute-start | bytes 138248 | tf_op jit(solution)/shard_map/ppermute | solution.py:20
  114.2 4.9 %collective-permute-start.3 = (bf16[6,10,1,384]{3,2,1,0:T(2,128)(2,1)}, bf16[6,10,1,384]{3,2,1,0:T(2,128)(2,1)S(1)}, u32[]{:S(2)}, u32[]{:S(2)}) collective-permute-start(bf16[6,10,1,384]{3,2,1,0:T(2,128)(2,1)} %get-tuple-element.47), channel_id=1, source_target_pairs={{0,1},{1,2},{2,3},{3,4},{4,5},{5,6},{6,7},{7,8},{8,9},{9,10},{10,1... | collective-permute-start | bytes 138248 | tf_op jit(solution)/shard_map/ppermute | solution.py:20
  119.1 2.1 collective-permute-start.4
  127.2 2.3 fusion.32
  129.4 1.8 reshape.211
  131.2 1.8 reshape.197
  133.0 1.8 reshape.199
  134.8 1.8 reshape.200
  136.6 1.8 reshape.202
  138.4 1.8 reshape.203
  140.2 1.8 reshape.205
  142.0 1.8 reshape.206
  143.8 1.8 reshape.208
  145.6 1.8 reshape.209
  151.7 24.5 %all-gather.7.cloned.1.call-done = bf16[27,384,384]{2,1,0:T(8,128)(2,1)} async-done(((bf16[27,96,384]{2,1,0:T(8,128)(2,1)}), bf16[27,384,384]{2,1,0:T(8,128)(2,1)}) %all-gather.7.cloned.1.call-update) | async-done | bytes 7962640 | tf_op jit(solution)/shard_map/all_gather | solution.py:59
  176.2 1.6 fusion.23
  177.8 1.8 fusion.24
  179.5 1.4 convolution_add_fusion.49
  181.0 1.5 convolution_add_fusion.48
  182.4 1.5 convolution_add_fusion.47
  183.9 1.3 convolution_add_fusion.46
  186.4 1.3 convolution_add_fusion.42
  194.3 3.3 collective-permute-start.5
  197.6 3.5 %collective-permute-done.5 = bf16[2,8,10,384]{3,2,1,0:T(8,128)(2,1)S(1)} collective-permute-done((bf16[2,8,10,384]{3,2,1,0:T(8,128)(2,1)S(1)}, bf16[2,8,10,384]{3,2,1,0:T(8,128)(2,1)S(1)}, u32[]{:S(2)}, u32[]{:S(2)}) %collective-permute-start.5) | collective-permute-done | bytes 122912 | tf_op jit(solution)/shard_map/ppermute | solution.py:10
  202.5 4.2 %collective-permute-start.6 = (bf16[6,1,10,384]{3,2,1,0:T(8,128)(2,1)S(1)}, bf16[6,1,10,384]{3,2,1,0:T(8,128)(2,1)S(1)}, u32[]{:S(2)}, u32[]{:S(2)}) collective-permute-start(bf16[6,1,10,384]{3,2,1,0:T(8,128)(2,1)S(1)} %get-tuple-element.65), channel_id=1, source_target_pairs={{0,16},{16,32},{32,48},{1,17},{17,33},{33,49},{2,18},{18,34},{34,5... | collective-permute-start | bytes 138248 | tf_op jit(solution)/shard_map/ppermute | solution.py:20
  210.1 5.8 %collective-permute-start.8 = (bf16[6,10,1,384]{3,2,1,0:T(2,128)(2,1)}, bf16[6,10,1,384]{3,2,1,0:T(2,128)(2,1)}, u32[]{:S(2)}, u32[]{:S(2)}) collective-permute-start(bf16[6,10,1,384]{3,2,1,0:T(2,128)(2,1)} %get-tuple-element.25), channel_id=1, source_target_pairs={{0,1},{1,2},{2,3},{3,4},{4,5},{5,6},{6,7},{7,8},{8,9},{9,10},{10,1... | collective-permute-start | bytes 138248 | tf_op jit(solution)/shard_map/ppermute | solution.py:20
  215.9 1.9 collective-permute-start.9
  220.1 42.1 %all-gather.11.cloned.1.call-done = bf16[27,384,384]{2,1,0:T(8,128)(2,1)} async-done(((bf16[27,96,384]{2,1,0:T(8,128)(2,1)}), bf16[27,384,384]{2,1,0:T(8,128)(2,1)}) %all-gather.11.cloned.1.call-update) | async-done | bytes 7962640 | tf_op jit(solution)/shard_map/all_gather | solution.py:59
  262.2 1.4 fusion.22
  263.6 1.8 reshape.232
  266.2 1.8 reshape.241
  268.8 1.8 reshape.249
  270.5 1.6 maximum_maximum_fusion.1
  272.1 1.8 fusion.30
  273.9 1.8 reshape.239
  275.7 1.9 fusion.31
  277.6 1.9 reshape.225
  279.4 1.8 reshape.227
  281.2 1.8 reshape.228
  283.0 1.8 reshape.230
  284.8 1.8 reshape.231
  286.6 1.8 reshape.233
  288.4 1.8 reshape.234
  290.1 1.8 reshape.236
  291.9 1.8 reshape.237
  293.7 1.8 reshape.240
  295.5 1.8 reshape.242
  297.3 1.8 reshape.243
  300.3 1.6 fusion.21
  301.9 1.4 convolution_add_fusion.24
  303.3 1.5 convolution_add_fusion.23
  304.8 1.5 convolution_add_fusion.22
  306.2 1.5 convolution_add_fusion.21
  307.7 1.6 convolution_add_fusion.20
  309.3 1.5 convolution_add_fusion.19
  310.8 1.5 convolution_add_fusion.18
  312.2 1.5 convolution_add_fusion.17
  313.7 1.3 convolution_add_fusion.16
  (186 shorter events, 42.7 us)
Async XLA Ops:
  6.5 90.8 %copy-start.1 = (bf16[4,8,10,384]{3,1,2,0:T(8,128)(2,1)S(1)}, bf16[4,8,10,384]{3,1,2,0:T(8,128)(2,1)}, u32[]{:S(2)}) copy-start(bf16[4,8,10,384]{3,1,2,0:T(8,128)(2,1)} %param.7) | copy-start | bytes 737284
  6.5 91.0 %copy-start.35 = (f32[384]{0:T(512)S(1)}, f32[384]{0:T(512)}, u32[]{:S(2)}) copy-start(f32[384]{0:T(512)} %param.8) | copy-start | bytes 4612
  6.5 46.8 %all-gather.5.cloned.1.call-start = ((), (), s32[]{:S(2)}) async-start(), calls=%async_computation | async-start | bytes 2506752 | tf_op jit(solution)/shard_map/all_gather | solution.py:57
  7.3 86.4 %all-gather.9.cloned.1.call-start = ((), (), s32[]{:S(2)}) async-start(), calls=%async_computation.2 | async-start | bytes 2506752 | tf_op jit(solution)/shard_map/all_gather | solution.py:57
  8.0 168.2 %all-gather.7.cloned.1.call-start = ((), (), s32[]{:S(2)}) async-start(), calls=%async_computation.1 | async-start | bytes 9953280 | tf_op jit(solution)/shard_map/all_gather | solution.py:59
  57.1 205.1 %all-gather.11.cloned.1.call-start = ((), (), s32[]{:S(2)}) async-start(), calls=%async_computation.3 | async-start | bytes 9953280 | tf_op jit(solution)/shard_map/all_gather | solution.py:59
  97.9 7.1 %collective-permute-start = (bf16[2,8,10,384]{3,2,1,0:T(8,128)(2,1)S(1)}, bf16[2,8,10,384]{3,2,1,0:T(8,128)(2,1)S(1)}, u32[]{:S(2)}, u32[]{:S(2)}) collective-permute-start(bf16[2,8,10,384]{3,2,1,0:T(8,128)(2,1)S(1)} %slice.512), channel_id=1, source_target_pairs={{0,64},{64,128},{128,192},{1,65},{65,129},{129,193},{2,66},{66,130... | collective-permute-start | bytes 368648 | tf_op jit(solution)/shard_map/ppermute | solution.py:10
  105.0 7.0 %collective-permute-start.2 = (bf16[6,1,10,384]{3,2,1,0:T(8,128)(2,1)S(1)}, bf16[6,1,10,384]{3,2,1,0:T(8,128)(2,1)S(1)}, u32[]{:S(2)}, u32[]{:S(2)}) collective-permute-start(bf16[6,1,10,384]{3,2,1,0:T(8,128)(2,1)S(1)} %get-tuple-element.72), channel_id=1, source_target_pairs={{16,0},{32,16},{48,32},{17,1},{33,17},{49,33},{18,2},{34,18},{50,3... | collective-permute-start | bytes 138248 | tf_op jit(solution)/shard_map/ppermute | solution.py:21
  106.3 7.0 %collective-permute-start.1 = (bf16[6,1,10,384]{3,2,1,0:T(8,128)(2,1)S(1)}, bf16[6,1,10,384]{3,2,1,0:T(8,128)(2,1)S(1)}, u32[]{:S(2)}, u32[]{:S(2)}) collective-permute-start(bf16[6,1,10,384]{3,2,1,0:T(8,128)(2,1)S(1)} %get-tuple-element.71), channel_id=1, source_target_pairs={{0,16},{16,32},{32,48},{1,17},{17,33},{33,49},{2,18},{18,34},{34,5... | collective-permute-start | bytes 138248 | tf_op jit(solution)/shard_map/ppermute | solution.py:20
  114.2 12.3 %collective-permute-start.3 = (bf16[6,10,1,384]{3,2,1,0:T(2,128)(2,1)}, bf16[6,10,1,384]{3,2,1,0:T(2,128)(2,1)S(1)}, u32[]{:S(2)}, u32[]{:S(2)}) collective-permute-start(bf16[6,10,1,384]{3,2,1,0:T(2,128)(2,1)} %get-tuple-element.47), channel_id=1, source_target_pairs={{0,1},{1,2},{2,3},{3,4},{4,5},{5,6},{6,7},{7,8},{8,9},{9,10},{10,1... | collective-permute-start | bytes 138248 | tf_op jit(solution)/shard_map/ppermute | solution.py:20
  119.1 7.4 %collective-permute-start.4 = (bf16[6,10,1,384]{3,2,1,0:T(2,128)(2,1)}, bf16[6,10,1,384]{3,2,1,0:T(2,128)(2,1)S(1)}, u32[]{:S(2)}, u32[]{:S(2)}) collective-permute-start(bf16[6,10,1,384]{3,2,1,0:T(2,128)(2,1)} %get-tuple-element.48), channel_id=1, source_target_pairs={{1,0},{2,1},{3,2},{4,3},{5,4},{6,5},{7,6},{8,7},{9,8},{10,9},{11,1... | collective-permute-start | bytes 138248 | tf_op jit(solution)/shard_map/ppermute | solution.py:21
  148.1 35.8 %copy-start.7 = (bf16[320,384]{1,0:T(8,128)(2,1)S(1)}, bf16[320,384]{1,0:T(8,128)(2,1)}, u32[]{:S(2)}) copy-start(bf16[320,384]{1,0:T(8,128)(2,1)} %reshape.201) | copy-start | bytes 737284
  148.9 37.1 %copy-start.14 = (bf16[320,384]{1,0:T(8,128)(2,1)S(1)}, bf16[320,384]{1,0:T(8,128)(2,1)}, u32[]{:S(2)}) copy-start(bf16[320,384]{1,0:T(8,128)(2,1)} %reshape.204) | copy-start | bytes 737284
  151.4 36.3 %copy-start.26 = (bf16[320,384]{1,0:T(8,128)(2,1)S(1)}, bf16[320,384]{1,0:T(8,128)(2,1)}, u32[]{:S(2)}) copy-start(bf16[320,384]{1,0:T(8,128)(2,1)} %reshape.206) | copy-start | bytes 737284
  151.5 33.8 %copy-start.31 = (bf16[320,384]{1,0:T(8,128)(2,1)S(1)}, bf16[320,384]{1,0:T(8,128)(2,1)}, u32[]{:S(2)}) copy-start(bf16[320,384]{1,0:T(8,128)(2,1)} %reshape.202) | copy-start | bytes 737284
  151.5 34.2 %copy-start.29 = (bf16[320,384]{1,0:T(8,128)(2,1)S(1)}, bf16[320,384]{1,0:T(8,128)(2,1)}, u32[]{:S(2)}) copy-start(bf16[320,384]{1,0:T(8,128)(2,1)} %reshape.203) | copy-start | bytes 737284
  176.2 9.1 %copy-start = (bf16[27,384,384]{2,1,0:T(8,128)(2,1)S(1)}, bf16[27,384,384]{2,1,0:T(8,128)(2,1)}, u32[]{:S(2)}) copy-start(bf16[27,384,384]{2,1,0:T(8,128)(2,1)} %all-gather.7.cloned.1.call-done) | copy-start | bytes 23887876
  176.2 11.9 %copy-start.12 = (bf16[320,384]{1,0:T(8,128)(2,1)S(1)}, bf16[320,384]{1,0:T(8,128)(2,1)}, u32[]{:S(2)}) copy-start(bf16[320,384]{1,0:T(8,128)(2,1)} %reshape.207) | copy-start | bytes 737284
  177.8 10.7 %copy-start.25 = (bf16[320,384]{1,0:T(8,128)(2,1)S(1)}, bf16[320,384]{1,0:T(8,128)(2,1)}, u32[]{:S(2)}) copy-start(bf16[320,384]{1,0:T(8,128)(2,1)} %reshape.208) | copy-start | bytes 737284
  181.0 7.8 %copy-start.23 = (bf16[320,384]{1,0:T(8,128)(2,1)S(1)}, bf16[320,384]{1,0:T(8,128)(2,1)}, u32[]{:S(2)}) copy-start(bf16[320,384]{1,0:T(8,128)(2,1)} %reshape.209) | copy-start | bytes 737284
  182.4 6.7 %copy-start.33 = (bf16[320,384]{1,0:T(8,128)(2,1)S(1)}, bf16[320,384]{1,0:T(8,128)(2,1)}, u32[]{:S(2)}) copy-start(bf16[320,384]{1,0:T(8,128)(2,1)} %reshape.210) | copy-start | bytes 737284
  183.9 5.6 %copy-start.20 = (bf16[320,384]{1,0:T(8,128)(2,1)S(1)}, bf16[320,384]{1,0:T(8,128)(2,1)}, u32[]{:S(2)}) copy-start(bf16[320,384]{1,0:T(8,128)(2,1)} %reshape.212) | copy-start | bytes 737284
  185.3 4.5 %copy-start.10 = (bf16[320,384]{1,0:T(8,128)(2,1)S(1)}, bf16[320,384]{1,0:T(8,128)(2,1)}, u32[]{:S(2)}) copy-start(bf16[320,384]{1,0:T(8,128)(2,1)} %reshape.213) | copy-start | bytes 737284
  185.7 4.5 %copy-start.18 = (bf16[320,384]{1,0:T(8,128)(2,1)S(1)}, bf16[320,384]{1,0:T(8,128)(2,1)}, u32[]{:S(2)}) copy-start(bf16[320,384]{1,0:T(8,128)(2,1)} %reshape.214) | copy-start | bytes 737284
  186.0 4.5 %copy-start.17 = (bf16[320,384]{1,0:T(8,128)(2,1)S(1)}, bf16[320,384]{1,0:T(8,128)(2,1)}, u32[]{:S(2)}) copy-start(bf16[320,384]{1,0:T(8,128)(2,1)} %reshape.215) | copy-start | bytes 737284
  186.4 4.5 %copy-start.8 = (bf16[320,384]{1,0:T(8,128)(2,1)S(1)}, bf16[320,384]{1,0:T(8,128)(2,1)}, u32[]{:S(2)}) copy-start(bf16[320,384]{1,0:T(8,128)(2,1)} %reshape.216) | copy-start | bytes 737284
  187.7 3.5 %copy-start.16 = (bf16[320,384]{1,0:T(8,128)(2,1)S(1)}, bf16[320,384]{1,0:T(8,128)(2,1)}, u32[]{:S(2)}) copy-start(bf16[320,384]{1,0:T(8,128)(2,1)} %reshape.217) | copy-start | bytes 737284
  188.1 3.5 %copy-start.15 = (bf16[320,384]{1,0:T(8,128)(2,1)S(1)}, bf16[320,384]{1,0:T(8,128)(2,1)}, u32[]{:S(2)}) copy-start(bf16[320,384]{1,0:T(8,128)(2,1)} %reshape.218) | copy-start | bytes 737284
  188.4 3.5 %copy-start.4 = (bf16[320,384]{1,0:T(8,128)(2,1)S(1)}, bf16[320,384]{1,0:T(8,128)(2,1)}, u32[]{:S(2)}) copy-start(bf16[320,384]{1,0:T(8,128)(2,1)} %reshape.219) | copy-start | bytes 737284
  189.5 3.5 %copy-start.5 = (bf16[320,384]{1,0:T(8,128)(2,1)S(1)}, bf16[320,384]{1,0:T(8,128)(2,1)}, u32[]{:S(2)}) copy-start(bf16[320,384]{1,0:T(8,128)(2,1)} %reshape.222) | copy-start | bytes 737284
  189.9 3.5 %copy-start.34 = (f32[384]{0:T(512)S(1)}, f32[384]{0:T(512)}, u32[]{:S(2)}) copy-start(f32[384]{0:T(512)} %param.10) | copy-start | bytes 4612
  190.2 3.8 %copy-start.36 = (f32[384]{0:T(512)S(1)}, f32[384]{0:T(512)}, u32[]{:S(2)}) copy-start(f32[384]{0:T(512)} %param.11) | copy-start | bytes 4612
  194.3 6.8 %collective-permute-start.5 = (bf16[2,8,10,384]{3,2,1,0:T(8,128)(2,1)S(1)}, bf16[2,8,10,384]{3,2,1,0:T(8,128)(2,1)S(1)}, u32[]{:S(2)}, u32[]{:S(2)}) collective-permute-start(bf16[2,8,10,384]{3,2,1,0:T(8,128)(2,1)S(1)} %slice.566), channel_id=1, source_target_pairs={{0,64},{64,128},{128,192},{1,65},{65,129},{129,193},{2,66},{66,130... | collective-permute-start | bytes 368648 | tf_op jit(solution)/shard_map/ppermute | solution.py:10
  201.2 7.2 %collective-permute-start.7 = (bf16[6,1,10,384]{3,2,1,0:T(8,128)(2,1)S(1)}, bf16[6,1,10,384]{3,2,1,0:T(8,128)(2,1)S(1)}, u32[]{:S(2)}, u32[]{:S(2)}) collective-permute-start(bf16[6,1,10,384]{3,2,1,0:T(8,128)(2,1)S(1)} %get-tuple-element.66), channel_id=1, source_target_pairs={{16,0},{32,16},{48,32},{17,1},{33,17},{49,33},{18,2},{34,18},{50,3... | collective-permute-start | bytes 138248 | tf_op jit(solution)/shard_map/ppermute | solution.py:21
  202.5 6.8 %collective-permute-start.6 = (bf16[6,1,10,384]{3,2,1,0:T(8,128)(2,1)S(1)}, bf16[6,1,10,384]{3,2,1,0:T(8,128)(2,1)S(1)}, u32[]{:S(2)}, u32[]{:S(2)}) collective-permute-start(bf16[6,1,10,384]{3,2,1,0:T(8,128)(2,1)S(1)} %get-tuple-element.65), channel_id=1, source_target_pairs={{0,16},{16,32},{32,48},{1,17},{17,33},{33,49},{2,18},{18,34},{34,5... | collective-permute-start | bytes 138248 | tf_op jit(solution)/shard_map/ppermute | solution.py:20
  210.1 60.4 %collective-permute-start.8 = (bf16[6,10,1,384]{3,2,1,0:T(2,128)(2,1)}, bf16[6,10,1,384]{3,2,1,0:T(2,128)(2,1)}, u32[]{:S(2)}, u32[]{:S(2)}) collective-permute-start(bf16[6,10,1,384]{3,2,1,0:T(2,128)(2,1)} %get-tuple-element.25), channel_id=1, source_target_pairs={{0,1},{1,2},{2,3},{3,4},{4,5},{5,6},{6,7},{7,8},{8,9},{9,10},{10,1... | collective-permute-start | bytes 138248 | tf_op jit(solution)/shard_map/ppermute | solution.py:20
  215.9 54.6 %collective-permute-start.9 = (bf16[6,10,1,384]{3,2,1,0:T(2,128)(2,1)}, bf16[6,10,1,384]{3,2,1,0:T(2,128)(2,1)}, u32[]{:S(2)}, u32[]{:S(2)}) collective-permute-start(bf16[6,10,1,384]{3,2,1,0:T(2,128)(2,1)} %get-tuple-element.26), channel_id=1, source_target_pairs={{1,0},{2,1},{3,2},{4,3},{5,4},{6,5},{7,6},{8,7},{9,8},{10,9},{11,1... | collective-permute-start | bytes 138248 | tf_op jit(solution)/shard_map/ppermute | solution.py:21
  277.6 22.3 %copy-start.3 = (bf16[4,8,10,384]{3,2,1,0:T(8,128)(2,1)S(1)}, bf16[4,8,10,384]{3,2,1,0:T(8,128)(2,1)}, u32[]{:S(2)}) copy-start(bf16[4,8,10,384]{3,2,1,0:T(8,128)(2,1)} %get-tuple-element.15) | copy-start | bytes 737284
  277.6 22.5 %copy-start.2 = (bf16[4,8,10,384]{3,2,1,0:T(8,128)(2,1)S(1)}, bf16[4,8,10,384]{3,2,1,0:T(8,128)(2,1)}, u32[]{:S(2)}) copy-start(bf16[4,8,10,384]{3,2,1,0:T(8,128)(2,1)} %get-tuple-element.14) | copy-start | bytes 737284
  299.9 13.8 %copy-start.30 = (bf16[320,384]{1,0:T(8,128)(2,1)S(1)}, bf16[320,384]{1,0:T(8,128)(2,1)}, u32[]{:S(2)}) copy-start(bf16[320,384]{1,0:T(8,128)(2,1)} %reshape.234) | copy-start | bytes 737284
  300.1 15.0 %copy-start.13 = (bf16[320,384]{1,0:T(8,128)(2,1)S(1)}, bf16[320,384]{1,0:T(8,128)(2,1)}, u32[]{:S(2)}) copy-start(bf16[320,384]{1,0:T(8,128)(2,1)} %reshape.235) | copy-start | bytes 737284
  300.3 16.1 %slice-start = ((s8[7962624]{0:T(1024)(128)(4,1)}), s8[4194304]{0:T(1024)(128)(4,1)S(1)}, s32[]{:S(2)}) async-start(s8[7962624]{0:T(1024)(128)(4,1)} %bitcast.217), calls=%async_computation.4 | async-start | bytes 8388608
  300.3 16.1 %copy-start.28 = (bf16[320,384]{1,0:T(8,128)(2,1)S(1)}, bf16[320,384]{1,0:T(8,128)(2,1)}, u32[]{:S(2)}) copy-start(bf16[320,384]{1,0:T(8,128)(2,1)} %reshape.236) | copy-start | bytes 737284
  303.3 13.4 %copy-start.27 = (bf16[320,384]{1,0:T(8,128)(2,1)S(1)}, bf16[320,384]{1,0:T(8,128)(2,1)}, u32[]{:S(2)}) copy-start(bf16[320,384]{1,0:T(8,128)(2,1)} %reshape.237) | copy-start | bytes 737284
  304.8 12.3 %copy-start.32 = (bf16[320,384]{1,0:T(8,128)(2,1)S(1)}, bf16[320,384]{1,0:T(8,128)(2,1)}, u32[]{:S(2)}) copy-start(bf16[320,384]{1,0:T(8,128)(2,1)} %reshape.238) | copy-start | bytes 737284
  306.2 11.2 %copy-start.24 = (bf16[320,384]{1,0:T(8,128)(2,1)S(1)}, bf16[320,384]{1,0:T(8,128)(2,1)}, u32[]{:S(2)}) copy-start(bf16[320,384]{1,0:T(8,128)(2,1)} %reshape.240) | copy-start | bytes 737284
  307.7 8.7 %slice-start.1 = ((s8[7962624]{0:T(1024)(128)(4,1)}), s8[3768320]{0:T(1024)(128)(4,1)S(1)}, s32[]{:S(2)}) async-start(s8[7962624]{0:T(1024)(128)(4,1)} %bitcast.217), calls=%async_computation.5 | async-start | bytes 7536640
  307.7 10.1 %copy-start.11 = (bf16[320,384]{1,0:T(8,128)(2,1)S(1)}, bf16[320,384]{1,0:T(8,128)(2,1)}, u32[]{:S(2)}) copy-start(bf16[320,384]{1,0:T(8,128)(2,1)} %reshape.241) | copy-start | bytes 737284
  309.3 8.9 %copy-start.22 = (bf16[320,384]{1,0:T(8,128)(2,1)S(1)}, bf16[320,384]{1,0:T(8,128)(2,1)}, u32[]{:S(2)}) copy-start(bf16[320,384]{1,0:T(8,128)(2,1)} %reshape.242) | copy-start | bytes 737284
  310.8 7.7 %copy-start.21 = (bf16[320,384]{1,0:T(8,128)(2,1)S(1)}, bf16[320,384]{1,0:T(8,128)(2,1)}, u32[]{:S(2)}) copy-start(bf16[320,384]{1,0:T(8,128)(2,1)} %reshape.243) | copy-start | bytes 737284
  312.2 6.6 %copy-start.9 = (bf16[320,384]{1,0:T(8,128)(2,1)S(1)}, bf16[320,384]{1,0:T(8,128)(2,1)}, u32[]{:S(2)}) copy-start(bf16[320,384]{1,0:T(8,128)(2,1)} %reshape.244) | copy-start | bytes 737284
  313.7 5.5 %copy-start.19 = (bf16[320,384]{1,0:T(8,128)(2,1)S(1)}, bf16[320,384]{1,0:T(8,128)(2,1)}, u32[]{:S(2)}) copy-start(bf16[320,384]{1,0:T(8,128)(2,1)} %reshape.245) | copy-start | bytes 737284
  317.8 3.3 copy-start.6
  318.5 3.3 %copy-start.37 = (f32[384]{0:T(512)S(1)}, f32[384]{0:T(512)}, u32[]{:S(2)}) copy-start(f32[384]{0:T(512)} %param.13) | copy-start | bytes 4612
Sparse Core Ops, SparseCore 0:
  9.2 44.1 all-gather.4
  55.2 38.3 all-gather.8
  95.4 80.7 all-gather.6
  177.9 84.2 all-gather.10
where the time goes:
time: 331 us; the launch traced here: 329 us
  waiting for transfers between devices  159 us (48%)
  local copies, waits for them, and re-layouts  79.1 us (24%)
  matrix products  39.5 us (12%)
  starting transfers between devices  32 us (10%)
  between operations  14.3 us (4%)
  other arithmetic  5.48 us (2%)
    all_gather x2, waiting for transfers between devices, convolve(): row_kernel = lax.all_gather(kernel, 'width', axis=1, tiled=True)  81.8 us
    all_gather x2, waiting for transfers between devices, convolve(): lax.all_gather(row_kernel, 'height', axis=1, tiled=True)  66.6 us
    reshape x53, local copies, waits for them, and re-layouts, fold_piece(): window.reshape(-1, count_in)  63 us
    dot_general x54, matrix products, fold_piece(): jnp.dot(window.reshape(-1, count_in), piece[9 * step_t + 3 * step_h + ste...  39.5 us
    ppermute x4, starting transfers between devices, extended(): before = lax.ppermute(last, axis, up)  18.9 us
    slice x6, local copies, waits for them, and re-layouts, fold_piece(): widened[step_t:step_t + frames, step_h:step_h + rows, step_w:step_w + cols]  7.5 us
    all_gather x2, local copies, waits for them, and re-layouts, convolve(): row_kernel = lax.all_gather(kernel, 'width', axis=1, tiled=True)  7.38 us
    ppermute x2, waiting for transfers between devices, passed_along(): return lax.ppermute(x, axis, pairs)  6.76 us
  transfers between devices with their start and end apart: 14, of which 8 were waited for; matrix products, arithmetic and copies ran while one was open for 22% of the time, Pallas kernels for 0%

commit v1 on v0

--- a/solution.py
+++ b/solution.py
@@ -51,13 +51,21 @@
 
 
 def convolve(widened, kernel, bias, frames, rows, cols):
+
+    def _press_sector(message, which_dim):
+        big = jax.lax.all_to_all(
+            jnp.stack([message for _ in range(jax.lax.axis_size("height"))], axis=0),
+            axis_name="height",
+            concat_axis=0,
+            split_axis=0,
+        )
+        return jnp.concatenate(big, axis=which_dim)
+
     out_chans = kernel.shape[2]
     empty = jnp.zeros((frames * rows * cols, out_chans), jnp.float32)
     fold_piece = make_folder(widened, frames, rows, cols)
     row_kernel = lax.all_gather(kernel, "width", axis=1, tiled=True)
-    total = fold_piece(
-        empty, lax.all_gather(row_kernel, "height", axis=1, tiled=True), jnp.int32(0)
-    )
+    total = fold_piece(empty, _press_sector(row_kernel, 1), jnp.int32(0))
     return total.reshape(frames, rows, cols, out_chans) + bias
 
 

time: 331 us -> 378 us (1.14)
  waiting for transfers between devices: 159 us -> 191 us
  local copies, waits for them, and re-layouts: 79.1 us -> 103 us
  matrix products: 39.5 us -> 20.1 us
  starting transfers between devices: 32 us -> 40.5 us
    ppermute x4, waiting for transfers between devices: 0.01 us -> 73.7 us  [extended(): after = lax.ppermute(first, axis, down)]
    all_gather x2 -> x0, waiting for transfers between devices: 66.6 us -> none  [convolve(): lax.all_gather(row_kernel, 'height', axis=1, tiled=True)]
    all_to_all x0 -> x2, waiting for transfers between devices: none -> 66.3 us  [_press_sector(): jax.lax.all_to_all(jnp.stack([message for _ in range(jax.lax.axis_size('h...]
    all_gather x2, waiting for transfers between devices: 81.8 us -> 46.1 us  [convolve(): row_kernel = lax.all_gather(kernel, 'width', axis=1, tiled=True)]
    dot_general x54, matrix products: 39.5 us -> 20.1 us  [fold_piece(): jnp.dot(window.reshape(-1, count_in), piece[9 * step_t + 3 * step_h + ste...]
    slice x0 -> x4, local copies, waits for them, and re-layouts: none -> 13.5 us  [fold_piece(): piece[9 * step_t + 3 * step_h + step_w]]
    all_to_all x0 -> x2, starting transfers between devices: none -> 11.4 us  [_press_sector(): jax.lax.all_to_all(jnp.stack([message for _ in range(jax.lax.axis_size('h...]
    unnamed x80 -> x168, local copies, waits for them, and re-layouts: 0.17 us -> 8.17 us
  transfers between devices with their start and end apart: 14 -> 14, of which waited for: 8 -> 5; matrix products, arithmetic and copies ran while one was open for 22% -> 18% of each run, Pallas kernels for 0% -> 0%
where the time goes in v1:
time: 378 us; the launch traced here: 375 us
  waiting for transfers between devices  191 us (51%)
  local copies, waits for them, and re-layouts  103 us (27%)
  starting transfers between devices  40.5 us (11%)
  matrix products  20.1 us (5%)
  between operations  14.4 us (4%)
  other arithmetic  6.38 us (2%)
    ppermute x4, waiting for transfers between devices, extended(): after = lax.ppermute(first, axis, down)  73.7 us
    all_to_all x2, waiting for transfers between devices, _press_sector(): jax.lax.all_to_all(jnp.stack([message for _ in range(jax.lax.axis_size('h...  66.3 us
    reshape x53, local copies, waits for them, and re-layouts, fold_piece(): window.reshape(-1, count_in)  60.4 us
    all_gather x2, waiting for transfers between devices, convolve(): row_kernel = lax.all_gather(kernel, 'width', axis=1, tiled=True)  46.1 us
    dot_general x54, matrix products, fold_piece(): jnp.dot(window.reshape(-1, count_in), piece[9 * step_t + 3 * step_h + ste...  20.1 us
    ppermute x4, starting transfers between devices, extended(): before = lax.ppermute(last, axis, up)  16.2 us
    slice x4, local copies, waits for them, and re-layouts, fold_piece(): piece[9 * step_t + 3 * step_h + step_w]  13.5 us
    all_to_all x2, starting transfers between devices, _press_sector(): jax.lax.all_to_all(jnp.stack([message for _ in range(jax.lax.axis_size('h...  11.4 us
  transfers between devices with their start and end apart: 14, of which 5 were waited for; matrix products, arithmetic and copies ran while one was open for 18% of the time, Pallas kernels for 0%

profile of v1, /device:TPU:1, one launch (start us, length us, event | category | flops | bytes accessed | tf_op | source)
XLA Modules:
  0.0 375.3 jit_solution(7004110574929730363)
XLA Ops:
  7.3 46.1 %all-gather.3.cloned.1.call-done = bf16[27,96,384]{2,0,1:T(8,128)(2,1)} async-done(((bf16[27,6,384]{2,0,1:T(8,128)(2,1)}), bf16[27,96,384]{2,0,1:T(8,128)(2,1)}) %all-gather.3.cloned.1.call-update) | async-done | bytes 1990672 | tf_op jit(solution)/shard_map/all_gather | solution.py:67
  53.4 2.4 copy.17
  55.7 3.8 %stack.4 = bf16[4,27,96,384]{3,2,1,0:T(8,128)(2,1)} broadcast(bf16[27,96,384]{2,1,0:T(8,128)(2,1)S(1)} %copy.17), dimensions={1,2,3} | broadcast | bytes 9953280 | tf_op jit(solution)/shard_map/stack | solution.py:57
  59.6 5.7 %all-to-all-start = ((bf16[4,27,96,384]{3,2,1,0:T(8,128)(2,1)}), bf16[4,27,96,384]{3,2,1,0:T(8,128)(2,1)}, u32[]{:S(2)}, u32[]{:S(2)}) async-start(bf16[4,27,96,384]{3,2,1,0:T(8,128)(2,1)} %stack.4), calls=%async_computation | async-start | bytes 15925248 | tf_op jit(solution)/shard_map/all_to_all | solution.py:56
  66.6 3.1 collective-permute-start
  69.7 0.8 reshape.340
  70.5 3.2 collective-permute-done
  73.7 1.3 collective-permute-start.2
  75.0 4.0 %collective-permute-start.1 = (bf16[6,1,10,384]{3,2,1,0:T(8,128)(2,1)S(1)}, bf16[6,1,10,384]{3,2,1,0:T(8,128)(2,1)S(1)}, u32[]{:S(2)}, u32[]{:S(2)}) collective-permute-start(bf16[6,1,10,384]{3,2,1,0:T(8,128)(2,1)S(1)} %get-tuple-element.125), channel_id=1, source_target_pairs={{0,16},{16,32},{32,48},{1,17},{17,33},{33,49},{2,18},{18,34},{34,5... | collective-permute-start | bytes 138248 | tf_op jit(solution)/shard_map/ppermute | solution.py:20
  79.2 0.8 reshape.322
  80.7 73.7 %collective-permute-done.2 = bf16[6,1,10,384]{3,2,1,0:T(8,128)(2,1)S(1)} collective-permute-done((bf16[6,1,10,384]{3,2,1,0:T(8,128)(2,1)S(1)}, bf16[6,1,10,384]{3,2,1,0:T(8,128)(2,1)S(1)}, u32[]{:S(2)}, u32[]{:S(2)}) %collective-permute-start.2) | collective-permute-done | bytes 46112 | tf_op jit(solution)/shard_map/ppermute | solution.py:21
  154.5 0.8 pad_maximum_fusion.13
  155.3 3.7 collective-permute-start.3
  159.0 1.9 collective-permute-start.4
  161.4 0.8 reshape.319
  162.2 0.8 reshape.325
  163.0 0.8 reshape.328
  166.2 1.5 maximum_maximum_fusion
  167.7 2.2 fusion.32
  169.9 1.8 reshape.332
  171.7 1.8 reshape.317
  173.4 1.8 reshape.320
  175.2 1.8 reshape.321
  177.0 1.8 reshape.323
  178.8 1.8 reshape.324
  180.5 1.8 reshape.326
  182.3 1.8 reshape.327
  184.1 1.8 reshape.329
  185.9 1.8 reshape.330
  188.5 0.8 reshape.335
  190.6 2.4 copy.18
  193.0 3.9 %stack.5 = bf16[4,27,96,384]{3,2,1,0:T(8,128)(2,1)} broadcast(bf16[27,96,384]{2,1,0:T(8,128)(2,1)S(1)} %copy.18), dimensions={1,2,3} | broadcast | bytes 9953280 | tf_op jit(solution)/shard_map/stack | solution.py:57
  196.8 5.7 %all-to-all-start.1 = ((bf16[4,27,96,384]{3,2,1,0:T(8,128)(2,1)}), bf16[4,27,96,384]{3,2,1,0:T(8,128)(2,1)}, u32[]{:S(2)}, u32[]{:S(2)}) async-start(bf16[4,27,96,384]{3,2,1,0:T(8,128)(2,1)} %stack.5), calls=%async_computation.1 | async-start | bytes 15925248 | tf_op jit(solution)/shard_map/all_to_all | solution.py:56
  202.5 3.4 fusion.28
  206.0 1.9 fusion.29
  221.0 3.1 collective-permute-start.5
  224.1 66.3 %all-to-all-done.1 = bf16[4,27,96,384]{3,2,1,0:T(8,128)(2,1)} async-done(((bf16[4,27,96,384]{3,2,1,0:T(8,128)(2,1)}), bf16[4,27,96,384]{3,2,1,0:T(8,128)(2,1)}, u32[]{:S(2)}, u32[]{:S(2)}) %all-to-all-start.1) | async-done | bytes 7962656 | tf_op jit(solution)/shard_map/all_to_all | solution.py:56
  290.4 5.1 %fusion.26 = (bf16[1,4,96,384]{3,2,0,1:T(8,128)(2,1)}, bf16[1,4,96,384]{3,2,0,1:T(8,128)(2,1)}, bf16[1,4,96,384]{3,2,0,1:T(8,128)(2,1)}, bf16[1,4,96,384]{3,2,0,...) fusion(bf16[27,4,96,384]{3,2,0,1:T(8,128)(2,1)} %bitcast.28), kind=kLoop, calls=%fused_computation.111 | loop fusion | bytes 11206656 | tf_op jit(solution)/shard_map/slice | solution.py:45
  295.5 3.0 fusion.27
  298.6 1.3 collective-permute-start.7
  299.9 4.0 %collective-permute-start.6 = (bf16[6,1,10,384]{3,2,1,0:T(8,128)(2,1)S(1)}, bf16[6,1,10,384]{3,2,1,0:T(8,128)(2,1)S(1)}, u32[]{:S(2)}, u32[]{:S(2)}) collective-permute-start(bf16[6,1,10,384]{3,2,1,0:T(8,128)(2,1)S(1)} %get-tuple-element.119), channel_id=1, source_target_pairs={{0,16},{16,32},{32,48},{1,17},{17,33},{33,49},{2,18},{18,34},{34,5... | collective-permute-start | bytes 138248 | tf_op jit(solution)/shard_map/ppermute | solution.py:20
  305.9 0.8 pad_maximum_fusion.9
  306.7 4.5 %collective-permute-start.8 = (bf16[6,10,1,384]{3,2,1,0:T(2,128)(2,1)}, bf16[6,10,1,384]{3,2,1,0:T(2,128)(2,1)}, u32[]{:S(2)}, u32[]{:S(2)}) collective-permute-start(bf16[6,10,1,384]{3,2,1,0:T(2,128)(2,1)} %get-tuple-element.79), channel_id=1, source_target_pairs={{0,1},{1,2},{2,3},{3,4},{4,5},{5,6},{6,7},{7,8},{8,9},{9,10},{10,1... | collective-permute-start | bytes 138248 | tf_op jit(solution)/shard_map/ppermute | solution.py:20
  311.3 2.1 collective-permute-start.9
  314.6 1.1 fusion.34
  316.3 1.8 reshape.354
  318.1 0.8 reshape.357
  318.9 1.8 reshape.363
  322.3 1.6 maximum_maximum_fusion.1
  323.8 1.8 fusion.30
  325.6 1.8 reshape.361
  327.4 1.8 fusion.31
  329.2 1.8 reshape.346
  331.1 1.8 reshape.349
  332.9 1.8 reshape.350
  335.5 1.8 reshape.353
  337.3 1.8 reshape.355
  339.1 1.8 reshape.356
  341.7 1.8 reshape.359
  343.5 1.8 reshape.362
  346.0 1.8 reshape.365
  347.9 0.8 reshape.367
  351.8 1.3 fusion.41
  353.1 1.3 convolution_add_fusion.24
  (277 shorter events, 45.0 us)
Async XLA Ops:
  6.5 46.8 %all-gather.3.cloned.1.call-start = ((), (), s32[]{:S(2)}) async-start(), calls=%async_computation.2 | async-start | bytes 2506752 | tf_op jit(solution)/shard_map/all_gather | solution.py:67
  59.6 6.4 %copy-start = (bf16[4,8,10,384]{3,1,2,0:T(8,128)(2,1)S(1)}, bf16[4,8,10,384]{3,1,2,0:T(8,128)(2,1)}, u32[]{:S(2)}) copy-start(bf16[4,8,10,384]{3,1,2,0:T(8,128)(2,1)} %param.7) | copy-start | bytes 737284
  59.6 6.6 %copy-start.81 = (f32[384]{0:T(512)S(1)}, f32[384]{0:T(512)}, u32[]{:S(2)}) copy-start(f32[384]{0:T(512)} %param.8) | copy-start | bytes 4612
  59.6 133.4 %all-to-all-start = ((bf16[4,27,96,384]{3,2,1,0:T(8,128)(2,1)}), bf16[4,27,96,384]{3,2,1,0:T(8,128)(2,1)}, u32[]{:S(2)}, u32[]{:S(2)}) async-start(bf16[4,27,96,384]{3,2,1,0:T(8,128)(2,1)} %stack.4), calls=%async_computation | async-start | bytes 15925248 | tf_op jit(solution)/shard_map/all_to_all | solution.py:56
  65.3 125.3 %all-gather.5.cloned.1.call-start = ((), (), s32[]{:S(2)}) async-start(), calls=%async_computation.3 | async-start | bytes 2506752 | tf_op jit(solution)/shard_map/all_gather | solution.py:67
  66.6 7.1 %collective-permute-start = (bf16[2,8,10,384]{3,2,1,0:T(8,128)(2,1)S(1)}, bf16[2,8,10,384]{3,2,1,0:T(8,128)(2,1)S(1)}, u32[]{:S(2)}, u32[]{:S(2)}) collective-permute-start(bf16[2,8,10,384]{3,2,1,0:T(8,128)(2,1)S(1)} %slice.566), channel_id=1, source_target_pairs={{0,64},{64,128},{128,192},{1,65},{65,129},{129,193},{2,66},{66,130... | collective-permute-start | bytes 368648 | tf_op jit(solution)/shard_map/ppermute | solution.py:10
  73.7 80.7 %collective-permute-start.2 = (bf16[6,1,10,384]{3,2,1,0:T(8,128)(2,1)S(1)}, bf16[6,1,10,384]{3,2,1,0:T(8,128)(2,1)S(1)}, u32[]{:S(2)}, u32[]{:S(2)}) collective-permute-start(bf16[6,1,10,384]{3,2,1,0:T(8,128)(2,1)S(1)} %get-tuple-element.126), channel_id=1, source_target_pairs={{16,0},{32,16},{48,32},{17,1},{33,17},{49,33},{18,2},{34,18},{50,3... | collective-permute-start | bytes 138248 | tf_op jit(solution)/shard_map/ppermute | solution.py:21
  75.0 79.4 %collective-permute-start.1 = (bf16[6,1,10,384]{3,2,1,0:T(8,128)(2,1)S(1)}, bf16[6,1,10,384]{3,2,1,0:T(8,128)(2,1)S(1)}, u32[]{:S(2)}, u32[]{:S(2)}) collective-permute-start(bf16[6,1,10,384]{3,2,1,0:T(8,128)(2,1)S(1)} %get-tuple-element.125), channel_id=1, source_target_pairs={{0,16},{16,32},{32,48},{1,17},{17,33},{33,49},{2,18},{18,34},{34,5... | collective-permute-start | bytes 138248 | tf_op jit(solution)/shard_map/ppermute | solution.py:20
  155.3 10.9 %collective-permute-start.3 = (bf16[6,10,1,384]{3,2,1,0:T(2,128)(2,1)}, bf16[6,10,1,384]{3,2,1,0:T(2,128)(2,1)S(1)}, u32[]{:S(2)}, u32[]{:S(2)}) collective-permute-start(bf16[6,10,1,384]{3,2,1,0:T(2,128)(2,1)} %get-tuple-element.101), channel_id=1, source_target_pairs={{0,1},{1,2},{2,3},{3,4},{4,5},{5,6},{6,7},{7,8},{8,9},{9,10},{10,1... | collective-permute-start | bytes 138248 | tf_op jit(solution)/shard_map/ppermute | solution.py:20
  159.0 7.1 %collective-permute-start.4 = (bf16[6,10,1,384]{3,2,1,0:T(2,128)(2,1)}, bf16[6,10,1,384]{3,2,1,0:T(2,128)(2,1)}, u32[]{:S(2)}, u32[]{:S(2)}) collective-permute-start(bf16[6,10,1,384]{3,2,1,0:T(2,128)(2,1)} %get-tuple-element.102), channel_id=1, source_target_pairs={{1,0},{2,1},{3,2},{4,3},{5,4},{6,5},{7,6},{8,7},{9,8},{10,9},{11,1... | collective-permute-start | bytes 138248 | tf_op jit(solution)/shard_map/ppermute | solution.py:21
  196.8 93.6 %all-to-all-start.1 = ((bf16[4,27,96,384]{3,2,1,0:T(8,128)(2,1)}), bf16[4,27,96,384]{3,2,1,0:T(8,128)(2,1)}, u32[]{:S(2)}, u32[]{:S(2)}) async-start(bf16[4,27,96,384]{3,2,1,0:T(8,128)(2,1)} %stack.5), calls=%async_computation.1 | async-start | bytes 15925248 | tf_op jit(solution)/shard_map/all_to_all | solution.py:56
  206.0 2.0 copy-start.74
  206.0 2.3 copy-start.62
  210.6 1.0 copy-start.40
  221.0 77.6 %collective-permute-start.5 = (bf16[2,8,10,384]{3,2,1,0:T(8,128)(2,1)S(1)}, bf16[2,8,10,384]{3,2,1,0:T(8,128)(2,1)S(1)}, u32[]{:S(2)}, u32[]{:S(2)}) collective-permute-start(bf16[2,8,10,384]{3,2,1,0:T(8,128)(2,1)S(1)} %slice.620), channel_id=1, source_target_pairs={{0,64},{64,128},{128,192},{1,65},{65,129},{129,193},{2,66},{66,130... | collective-permute-start | bytes 368648 | tf_op jit(solution)/shard_map/ppermute | solution.py:10
  298.6 7.0 %collective-permute-start.7 = (bf16[6,1,10,384]{3,2,1,0:T(8,128)(2,1)S(1)}, bf16[6,1,10,384]{3,2,1,0:T(8,128)(2,1)S(1)}, u32[]{:S(2)}, u32[]{:S(2)}) collective-permute-start(bf16[6,1,10,384]{3,2,1,0:T(8,128)(2,1)S(1)} %get-tuple-element.120), channel_id=1, source_target_pairs={{16,0},{32,16},{48,32},{17,1},{33,17},{49,33},{18,2},{34,18},{50,3... | collective-permute-start | bytes 138248 | tf_op jit(solution)/shard_map/ppermute | solution.py:21
  299.9 6.0 %collective-permute-start.6 = (bf16[6,1,10,384]{3,2,1,0:T(8,128)(2,1)S(1)}, bf16[6,1,10,384]{3,2,1,0:T(8,128)(2,1)S(1)}, u32[]{:S(2)}, u32[]{:S(2)}) collective-permute-start(bf16[6,1,10,384]{3,2,1,0:T(8,128)(2,1)S(1)} %get-tuple-element.119), channel_id=1, source_target_pairs={{0,16},{16,32},{32,48},{1,17},{17,33},{33,49},{2,18},{18,34},{34,5... | collective-permute-start | bytes 138248 | tf_op jit(solution)/shard_map/ppermute | solution.py:20
  306.7 15.5 %collective-permute-start.8 = (bf16[6,10,1,384]{3,2,1,0:T(2,128)(2,1)}, bf16[6,10,1,384]{3,2,1,0:T(2,128)(2,1)}, u32[]{:S(2)}, u32[]{:S(2)}) collective-permute-start(bf16[6,10,1,384]{3,2,1,0:T(2,128)(2,1)} %get-tuple-element.79), channel_id=1, source_target_pairs={{0,1},{1,2},{2,3},{3,4},{4,5},{5,6},{6,7},{7,8},{8,9},{9,10},{10,1... | collective-permute-start | bytes 138248 | tf_op jit(solution)/shard_map/ppermute | solution.py:20
  311.3 11.0 %collective-permute-start.9 = (bf16[6,10,1,384]{3,2,1,0:T(2,128)(2,1)}, bf16[6,10,1,384]{3,2,1,0:T(2,128)(2,1)}, u32[]{:S(2)}, u32[]{:S(2)}) collective-permute-start(bf16[6,10,1,384]{3,2,1,0:T(2,128)(2,1)} %get-tuple-element.80), channel_id=1, source_target_pairs={{1,0},{2,1},{3,2},{4,3},{5,4},{6,5},{7,6},{8,7},{9,8},{10,9},{11,1... | collective-permute-start | bytes 138248 | tf_op jit(solution)/shard_map/ppermute | solution.py:21
  314.6 1.1 copy-start.32
  314.6 1.4 copy-start.76
  316.3 5.2 %copy-start.6 = (bf16[4,8,10,384]{3,2,1,0:T(8,128)(2,1)S(1)}, bf16[4,8,10,384]{3,2,1,0:T(8,128)(2,1)}, u32[]{:S(2)}) copy-start(bf16[4,8,10,384]{3,2,1,0:T(8,128)(2,1)} %get-tuple-element.103) | copy-start | bytes 737284
  329.2 5.5 %copy-start.5 = (bf16[4,8,10,384]{3,2,1,0:T(8,128)(2,1)S(1)}, bf16[4,8,10,384]{3,2,1,0:T(8,128)(2,1)}, u32[]{:S(2)}) copy-start(bf16[4,8,10,384]{3,2,1,0:T(8,128)(2,1)} %get-tuple-element.66) | copy-start | bytes 737284
  332.9 8.0 %copy-start.2 = (bf16[4,8,10,384]{3,2,1,0:T(8,128)(2,1)S(1)}, bf16[4,8,10,384]{3,2,1,0:T(8,128)(2,1)}, u32[]{:S(2)}) copy-start(bf16[4,8,10,384]{3,2,1,0:T(8,128)(2,1)} %get-tuple-element.64) | copy-start | bytes 737284
  337.3 8.0 %copy-start.1 = (bf16[4,8,10,384]{3,2,1,0:T(8,128)(2,1)S(1)}, bf16[4,8,10,384]{3,2,1,0:T(8,128)(2,1)}, u32[]{:S(2)}) copy-start(bf16[4,8,10,384]{3,2,1,0:T(8,128)(2,1)} %get-tuple-element.62) | copy-start | bytes 737284
  345.3 5.0 %copy-start.3 = (bf16[4,8,10,384]{3,2,1,0:T(8,128)(2,1)S(1)}, bf16[4,8,10,384]{3,2,1,0:T(8,128)(2,1)}, u32[]{:S(2)}) copy-start(bf16[4,8,10,384]{3,2,1,0:T(8,128)(2,1)} %get-tuple-element.68) | copy-start | bytes 737284
  346.0 2.6 copy-start.4
  348.7 3.1 copy-start.24
  349.5 3.6 copy-start.31
  351.0 3.5 copy-start.30
  351.0 3.5 copy-start.73
  353.1 1.7 copy-start.29
  353.1 1.7 copy-start.72
  354.5 1.0 copy-start.42
  354.9 1.0 copy-start.27
  354.9 1.1 copy-start.71
  355.5 1.0 copy-start.26
  355.5 1.1 copy-start.70
  356.0 1.0 copy-start.25
  356.0 1.1 copy-start.48
  356.6 1.0 copy-start.23
  356.6 1.1 copy-start.69
  357.0 1.0 copy-start.22
  357.0 1.1 copy-start.68
  357.7 1.1 copy-start.46
  358.1 1.1 copy-start.67
  358.7 1.0 copy-start.19
  358.7 1.1 copy-start.66
  359.2 1.0 copy-start.18
  359.2 1.1 copy-start.78
  359.8 1.1 copy-start.65
  360.3 1.0 copy-start.16
  360.3 1.1 copy-start.43
  360.9 1.1 copy-start.64
  361.3 1.1 copy-start.63
  362.0 1.1 copy-start.41
  362.4 1.1 copy-start.59
  363.0 1.1 copy-start.58
  364.5 1.0 copy-start.56
  364.9 1.0 copy-start.9
  365.0 1.1 copy-start.55
  365.5 1.1 copy-start.38
  366.0 1.0 copy-start.7
  366.0 1.1 copy-start.53
  (34 other events, 32.7 us)
Sparse Core Ops, SparseCore 0:
  9.2 44.1 all-gather.2
  67.9 38.7 all-gather.4
